TPU v7x, 32 devices: a whole 2x2x4 slice. The times are simulated.
32 devices in a mesh: grp: 4 (over y, core), loc: 8 (over z, x).
Axes of the slice: x: 2, y: 2, z: 4, core: 2. Of those that a mesh axis runs over, the one named last changes fastest.
Arguments:
- cavity_field: float32 [2, 256, 65536], P(None, ('grp', 'loc')), may hold values from -6 to 6
- direction: float32 [2, 2, 256, 65536], P(None, None, ('grp', 'loc')), may hold values from -6 to 6
- mode_degree: int32 [256], P(('grp', 'loc')), may hold values from 0 to 30
Outputs:
- preconditioned_product: float32 [2, 2, 256, 65536], P(None, None, ('grp', 'loc'))
All inputs are finite; a program needn't handle non-finite values.
Results may differ from a plain program's by a relative error of at most 0.0043.
Values may be sent and summed in bfloat16 or wider, within the bound.
A program may use at most 256 MiB of HBM per device.

v0:
```python
import functools
import math

import jax
import jax.numpy as jnp
import numpy as np
from jax import lax
from jax.experimental import pallas as pl
from jax.experimental.pallas import tpu as pltpu
from jax.sharding import PartitionSpec as P

MP = 16
MQ = 16
GSIDE = 64
NODES = 32
LEN = 256

DETUNE = 4.0
BETA_STEP = 2.0
DISPERSION = 80.0
KERR_GAIN = 8.0

CHUNKS = 2
AXES = ("grp", "loc")
MIB = 1 << 20


def node_table():
    spacing = 16.0 / GSIDE
    position = (np.arange(GSIDE) - (GSIDE - 1) / 2.0) * spacing
    root = spacing * np.exp(-position * position)
    basis = [root / np.linalg.norm(root)]
    diag, off = [], []
    for k in range(NODES):
        vec = position * basis[k]
        diag.append(vec @ basis[k])
        for _ in range(3):
            for prev in basis:
                vec = vec - (prev @ vec) * prev
        off.append(np.linalg.norm(vec))
        basis.append(vec / off[-1])
    jacobi = np.diag(diag) + np.diag(off[:-1], 1) + np.diag(off[:-1], -1)
    nodes, vectors = np.linalg.eigh(jacobi)
    weights = (root @ root) * vectors[0] ** 2
    nodes = 0.5 * (nodes - nodes[::-1])
    weights = 0.5 * (weights + weights[::-1])
    poly = [np.full(NODES, math.pi ** (-0.25)), math.sqrt(2.0) * nodes * math.pi ** (-0.25)]
    for degree in range(1, max(MP, MQ) - 1):
        poly.append(
            math.sqrt(2.0 / (degree + 1)) * nodes * poly[degree]
            - math.sqrt(degree / (degree + 1.0)) * poly[degree - 1]
        )
    side = np.stack(poly, 1) * (weights**0.25)[:, None]
    full = side[:, None, :MP, None] * side[None, :, None, :MQ]
    return full.reshape(NODES * NODES, MP * MQ)


def prep_kernel(chunks, dests, field_ref, dir_ref, *out_refs):
    span = field_ref.shape[2] // dests
    part = span // chunks
    for d in range(dests):
        for j in range(chunks):
            where = pl.ds(d * span + j * part, part)
            for c in range(2):
                out_refs[j][d, c] = field_ref[c, :, where].astype(jnp.bfloat16)
                for e in range(dir_ref.shape[0]):
                    out_refs[j][d, 2 + 2 * e + c] = dir_ref[e, c, :, where].astype(jnp.bfloat16)


def prep(cavity_field, direction, devices, chunks):
    dirs, _, modes, time_all = direction.shape
    sets = 2 * (dirs + 1)
    span = time_all // devices
    dests = 4
    part = span // chunks
    return pl.pallas_call(
        functools.partial(prep_kernel, chunks, dests),
        grid=(devices // dests,),
        in_specs=[
            pl.BlockSpec((2, modes, dests * span), lambda i: (0, 0, i)),
            pl.BlockSpec((dirs, 2, modes, dests * span), lambda i: (0, 0, 0, i)),
        ],
        out_specs=[pl.BlockSpec((dests, sets, modes, part), lambda i: (i, 0, 0, 0))] * chunks,
        out_shape=[jax.ShapeDtypeStruct((devices, sets, modes, part), jnp.bfloat16)] * chunks,
        compiler_params=pltpu.CompilerParams(vmem_limit_bytes=40 * MIB),
        name="prep",
    )(cavity_field, direction)


def halves(values):
    high = values.astype(jnp.bfloat16)
    return high, (values - high.astype(jnp.float32)).astype(jnp.bfloat16)


def dot16(left, right):
    return jnp.dot(left, right, preferred_element_type=jnp.float32)


def kerr_kernel(table_ref, back_ref, x_ref, out_ref):
    groups, sets, rows, cols = x_ref.shape
    modes = groups * rows
    points = table_ref.shape[1]
    step = 256
    planes = [
        x_ref[:, s].astype(jnp.float32).reshape(modes, cols).astype(jnp.bfloat16)
        for s in range(sets)
    ]
    dirs = sets // 2 - 1
    totals = [jnp.zeros((modes, cols), jnp.float32) for _ in range(2 * dirs)]
    for g in range(0, points, step):
        at = slice(g, g + step)
        vals = [dot16(table_ref[0, at, :], p) + dot16(table_ref[1, at, :], p) for p in planes]
        u_real, u_imag = vals[0], vals[1]
        real_sq = u_real * u_real
        imag_sq = u_imag * u_imag
        lead = 3.0 * real_sq + imag_sq
        tail = real_sq + 3.0 * imag_sq
        cross = 2.0 * u_real * u_imag
        back_high, back_low = back_ref[0, :, at], back_ref[1, :, at]
        for e in range(dirs):
            w_real, w_imag = vals[2 + 2 * e], vals[3 + 2 * e]
            jac = (lead * w_real + cross * w_imag, cross * w_real + tail * w_imag)
            for c in range(2):
                high, low = halves(jac[c])
                totals[2 * e + c] += (
                    dot16(back_high, high) + dot16(back_low, high) + dot16(back_high, low)
                )
    for e in range(dirs):
        out_ref[:, 2 * e, 0] = (
            (-KERR_GAIN * totals[2 * e + 1]).reshape(groups, rows, cols).astype(jnp.bfloat16)
        )
        out_ref[:, 2 * e + 1, 0] = (
            (KERR_GAIN * totals[2 * e]).reshape(groups, rows, cols).astype(jnp.bfloat16)
        )


def kerr(table, back, x):
    groups, sets, rows, cols = x.shape
    _, points, modes = table.shape
    blocks = cols // LEN
    outs = sets - 2
    return pl.pallas_call(
        kerr_kernel,
        grid=(blocks,),
        in_specs=[
            pl.BlockSpec((2, points, modes), lambda i: (0, 0, 0)),
            pl.BlockSpec((2, modes, points), lambda i: (0, 0, 0)),
            pl.BlockSpec((groups, sets, rows, LEN), lambda i: (0, 0, 0, i)),
        ],
        out_specs=pl.BlockSpec((groups, outs, 1, rows, LEN), lambda i: (0, 0, i, 0, 0)),
        out_shape=jax.ShapeDtypeStruct((groups, outs, blocks, rows, LEN), jnp.bfloat16),
        compiler_params=pltpu.CompilerParams(vmem_limit_bytes=40 * MIB),
        cost_estimate=pl.CostEstimate(
            flops=2 * (2 * sets + 3 * outs) * points * modes * cols,
            bytes_accessed=2 * (sets + outs) * modes * cols,
            transcendentals=0,
        ),
        name="kerr",
    )(table, back, x)


def split_table(values):
    high = np.asarray(values, jnp.bfloat16)
    low = np.asarray(values - high.astype(np.float64), jnp.bfloat16)
    return jnp.asarray(np.stack([high, low]))


def dot_left(table_ref, values):
    high, low = halves(values)
    return dot16(table_ref[0], high) + dot16(table_ref[1], high) + dot16(table_ref[0], low)


def dot_right(values, table_ref):
    high, low = halves(values)
    return dot16(high, table_ref[0]) + dot16(high, table_ref[1]) + dot16(low, table_ref[0])


def filter_kernel(chunks, degree_ref, left_ref, right_ref, left_inv_ref, right_inv_ref, twc_ref, tws_ref, disp_ref,
                  dir_ref, *rest):
    kerr_refs = rest[:chunks]
    out_ref, wide, rows = rest[chunks:]
    modes = dir_ref.shape[2]
    sources, _, blocks = kerr_refs[0].shape[:3]
    mode = pl.program_id(1)

    @pl.when(mode == 0)
    def _():
        def gather(src, carry):
            for j in range(chunks):
                for c in range(2):
                    for b in range(blocks):
                        at = (src * chunks + j) * blocks + b
                        lanes = pl.ds(pl.multiple_of(at * LEN, LEN), LEN)
                        wide[c, at] = dir_ref[0, c, :, lanes] + kerr_refs[j][src, c, b].astype(jnp.float32)
            return carry

        lax.fori_loop(0, sources, gather, 0)
        for m in range(modes):
            for c in range(2):
                rows[c, m] = wide[c, :, m, :]

    tw_cos = twc_ref[...]
    tw_sin = tws_ref[...]
    pair = jnp.concatenate([rows[0, mode], rows[1, mode]], 0)
    step = dot_left(left_ref, pair)
    step_real, step_imag = step[:LEN], step[LEN:]
    turned = jnp.concatenate(
        [
            step_real * tw_cos + step_imag * tw_sin,
            step_imag * tw_cos - step_real * tw_sin,
        ],
        1,
    )
    spec = dot_right(turned, right_ref)
    spec_real, spec_imag = spec[:, :LEN], spec[:, LEN:]
    phase = disp_ref[...] - BETA_STEP * degree_ref[mode].astype(jnp.float32)
    scale = (1.0 / (LEN * LEN)) / (4.0 + phase * phase)
    inv_real = 2.0 * scale
    inv_imag = -phase * scale
    mixed = jnp.concatenate(
        [
            inv_real * spec_real - inv_imag * spec_imag,
            inv_real * spec_imag + inv_imag * spec_real,
        ],
        1,
    )
    back = dot_right(mixed, right_inv_ref)
    back_real, back_imag = back[:, :LEN], back[:, LEN:]
    unturned = jnp.concatenate(
        [
            back_real * tw_cos - back_imag * tw_sin,
            back_imag * tw_cos + back_real * tw_sin,
        ],
        0,
    )
    done = dot_left(left_inv_ref, unturned)
    rows[0, mode] = done[:LEN]
    rows[1, mode] = done[LEN:]

    @pl.when(mode == modes - 1)
    def _():
        for m in range(modes):
            for c in range(2):
                wide[c, :, m, :] = rows[c, m]

        def scatter(i, carry):
            for b in range(8):
                at = i * 8 + b
                lanes = pl.ds(pl.multiple_of(at * LEN, LEN), LEN)
                for c in range(2):
                    out_ref[0, c, :, lanes] = wide[c, at] - dir_ref[0, c, :, lanes]
            return carry

        lax.fori_loop(0, LEN // 8, scatter, 0)


def filter_tables():
    idx = np.arange(LEN)
    angles = 2.0 * np.pi / LEN * (idx[:, None] * idx[None, :] % LEN)
    cos, sin = np.cos(angles), np.sin(angles)
    left = np.block([[cos, sin], [-sin, cos]])
    right = np.block([[cos, -sin], [sin, cos]])
    turn = 2.0 * np.pi / (LEN * LEN) * (idx[:, None] * idx[None, :])
    frequency = idx[:, None] + LEN * idx[None, :]
    half = LEN * LEN // 2
    kappa = np.where(frequency < half, frequency, frequency - 2 * half) / half
    mats = [split_table(t) for t in (left, right, right, left)]
    rest = [np.cos(turn), np.sin(turn), DETUNE + DISPERSION * kappa * kappa]
    return mats + [jnp.asarray(t, jnp.float32) for t in rest]


def precondition(mode_degree, direction, kerr_parts):
    dirs, _, modes, time_all = direction.shape
    chunks = len(kerr_parts)
    sources, _, blocks = kerr_parts[0].shape[:3]
    big = pl.BlockSpec((2, 2 * LEN, 2 * LEN), lambda e, m: (0, 0, 0))
    small = pl.BlockSpec((LEN, LEN), lambda e, m: (0, 0))
    wave = pl.BlockSpec((1, 2, modes, time_all), lambda e, m: (e, 0, 0, 0))
    part = pl.BlockSpec((sources, 2, blocks, modes, LEN), lambda e, m: (0, e, 0, 0, 0))
    return pl.pallas_call(
        functools.partial(filter_kernel, chunks),
        grid=(dirs, modes),
        in_specs=[pl.BlockSpec(memory_space=pltpu.SMEM)]
        + [big] * 4
        + [small] * 3
        + [wave]
        + [part] * chunks,
        out_specs=wave,
        out_shape=jax.ShapeDtypeStruct(direction.shape, jnp.float32),
        scratch_shapes=[
            pltpu.VMEM((2, LEN, modes, LEN), jnp.float32),
            pltpu.VMEM((2, modes, LEN, LEN), jnp.float32),
        ],
        compiler_params=pltpu.CompilerParams(vmem_limit_bytes=56 * MIB),
        name="precondition",
    )(mode_degree, *filter_tables(), direction, *kerr_parts)


def local(devices, cavity_field, direction, mode_degree):
    modes = direction.shape[2]
    table = node_table()
    forward = split_table(table)
    back = split_table(table.T)
    fold = max(1, 8 // modes)
    kerr_parts = []
    for x in prep(cavity_field, direction, devices, CHUNKS):
        x = lax.all_to_all(x, AXES, split_axis=0, concat_axis=0, tiled=True)
        if fold > 1:
            n, sets, r, cols = x.shape
            x = x.reshape(n // fold, fold, sets, r, cols).transpose(0, 2, 1, 3, 4)
            x = x.reshape(n // fold, sets, fold * r, cols)
        y = kerr(forward, back, x)
        if fold > 1:
            n, outs, blocks, r, cols = y.shape
            y = y.reshape(n, outs, blocks, fold, r // fold, cols).transpose(0, 3, 1, 2, 4, 5)
            y = y.reshape(n * fold, outs, blocks, r // fold, cols)
        kerr_parts.append(lax.all_to_all(y, AXES, split_axis=0, concat_axis=0, tiled=True))
    return precondition(mode_degree, direction, kerr_parts)


def solution(mesh):
    placed = (P(None, AXES, None), P(None, None, AXES, None), P(AXES))
    return jax.shard_map(
        functools.partial(local, mesh.size),
        mesh=mesh,
        in_specs=placed,
        out_specs=P(None, None, AXES, None),
        check_vma=False,
    )
```

profile of v0, /device:TPU:0, one launch (start us, length us, event | category | flops | bytes accessed | tf_op | source)
XLA Modules:
  0.0 331.9 jit_solution(14156957945472648329)
XLA Ops:
  0.0 0.0 copy-start
  0.0 2.2 copy-done
  2.2 5.9 %prep.1 = (bf16[32,6,8,1024]{3,2,1,0:T(8,128)(2,1)S(1)}, bf16[32,6,8,1024]{3,2,1,0:T(8,128)(2,1)S(1)}) custom-call(f32[2,8,65536]{2,1,0:T(8,128)S(1)} %copy-done, f32[2,2,8,65536]{3,2,1,0:T(8,128)} %dir_ref.3), custom_call_target="tpu_custom_call" | custom-call | tf_op jit(solution)/shard_map/prep/pallas_call | solution.py:76
  8.1 0.0 copy-start.1
  8.1 79.7 %all_to_all.20.x_ref = bf16[32,6,8,1024]{3,2,1,0:T(8,128)(2,1)} all-to-all(bf16[32,6,8,1024]{3,2,1,0:T(8,128)(2,1)S(1)} %get-tuple-element.7), channel_id=1, replica_groups=mesh['grp'=4,'loc'=8] {'grp','loc'}, dimensions={0} | all-to-all | bytes 6291456 | tf_op jit(solution)/shard_map/all_to_all | solution.py:307
  87.9 0.0 copy-done.1
  87.9 2.8 all-to-all-start.2
  90.7 0.0 copy-start.2
  90.7 1.9 copy-done.2
  92.6 0.0 copy-start.5
  92.6 1.2 copy-done.5
  93.8 0.0 copy-start.7
  93.8 1.2 copy-done.7
  95.0 14.9 %kerr.2 = bf16[32,4,4,8,256]{4,3,2,1,0:T(8,128)(2,1)S(1)} custom-call(bf16[2,1024,256]{2,1,0:T(8,128)(2,1)S(1)} %copy-done.7, bf16[2,256,1024]{2,1,0:T(8,128)(2,1)S(1)} %copy-done.5, bf16[32,6,8,1024]{3,2,1,0:T(8,128)(2,1)S(1)} %copy-done.2), custom_call_target="tpu_custom_call" | custom-call | flops 12884901888 | bytes 5242880 | tf_op jit(solution)/shard_map/kerr/pallas_call | solution.py:142
  109.9 0.0 copy-start.3
  109.9 1.3 copy-done.3
  111.2 52.1 %all-to-all-done.2.x_ref = bf16[32,6,8,1024]{3,2,1,0:T(8,128)(2,1)S(1)} async-done(((bf16[32,6,8,1024]{3,2,1,0:T(8,128)(2,1)}), bf16[32,6,8,1024]{3,2,1,0:T(8,128)(2,1)S(1)}, u32[]{:S(2)}, u32[]{:S(2)}) %all-to-all-start.2) | async-done | bytes 3145760 | tf_op jit(solution)/shard_map/all_to_all | solution.py:307
  163.3 3.5 %all-to-all-start.1 = ((bf16[32,4,4,8,256]{4,3,2,1,0:T(8,128)(2,1)}), bf16[32,4,4,8,256]{4,3,2,1,0:T(8,128)(2,1)}, u32[]{:S(2)}, u32[]{:S(2)}) async-start(bf16[32,4,4,8,256]{4,3,2,1,0:T(8,128)(2,1)} %copy-done.3), calls=%async_computation.1 | async-start | bytes 4194304 | tf_op jit(solution)/shard_map/all_to_all | solution.py:317
  166.8 0.0 copy-start.6
  166.8 1.2 copy-done.6
  168.1 0.0 copy-start.8
  168.1 1.2 copy-done.8
  169.3 14.9 %kerr.3 = bf16[32,4,4,8,256]{4,3,2,1,0:T(8,128)(2,1)S(1)} custom-call(bf16[2,1024,256]{2,1,0:T(8,128)(2,1)S(1)} %copy-done.8, bf16[2,256,1024]{2,1,0:T(8,128)(2,1)S(1)} %copy-done.6, bf16[32,6,8,1024]{3,2,1,0:T(8,128)(2,1)S(1)} %all-to-all-done.2.x_ref), custom_call_target="tpu_custom_call" | custom-call | flops 12884901888 | bytes 5242880 | tf_op jit(solution)/shard_map/kerr/pallas_call | solution.py:142
  184.1 0.0 copy-start.4
  184.2 1.3 copy-done.4
  185.5 31.4 %all-to-all-done.1.rest_0_ = bf16[32,4,4,8,256]{4,3,2,1,0:T(8,128)(2,1)} async-done(((bf16[32,4,4,8,256]{4,3,2,1,0:T(8,128)(2,1)}), bf16[32,4,4,8,256]{4,3,2,1,0:T(8,128)(2,1)}, u32[]{:S(2)}, u32[]{:S(2)}) %all-to-all-start.1) | async-done | bytes 2097184 | tf_op jit(solution)/shard_map/all_to_all | solution.py:317
  216.9 53.5 %all_to_all.21.rest_1_ = bf16[32,4,4,8,256]{4,3,2,1,0:T(8,128)(2,1)} all-to-all(bf16[32,4,4,8,256]{4,3,2,1,0:T(8,128)(2,1)} %copy-done.4), channel_id=1, replica_groups=mesh['grp'=4,'loc'=8] {'grp','loc'}, dimensions={0} | all-to-all | bytes 4194304 | tf_op jit(solution)/shard_map/all_to_all | solution.py:317
  270.4 61.6 %precondition.1 = f32[2,2,8,65536]{3,2,1,0:T(8,128)} custom-call(s32[8]{0:T(128)} %degree_ref.1, bf16[2,512,512]{2,1,0:T(8,128)(2,1)} %constant.16.clone.left_ref.right_inv_ref, bf16[2,512,512]{2,1,0:T(8,128)(2,1)} %constant.17.clone.right_ref.left_inv_ref, bf16[2,512,512]{2,1,0:T(8,128)(2,1)} %constant.17.clone.right_ref.left_inv_ref, ...), custom_call_target="tpu_custom_call" | custom-call | tf_op jit(solution)/shard_map/precondition/pallas_call | solution.py:280
Async XLA Ops:
  0.0 2.2 copy-start
  8.1 79.8 %copy-start.1 = (bf16[32,6,8,1024]{3,2,1,0:T(8,128)(2,1)}, bf16[32,6,8,1024]{3,2,1,0:T(8,128)(2,1)S(1)}, u32[]{:S(2)}) copy-start(bf16[32,6,8,1024]{3,2,1,0:T(8,128)(2,1)S(1)} %get-tuple-element.8) | copy-start | bytes 9437188
  87.9 75.4 %all-to-all-start.2 = ((bf16[32,6,8,1024]{3,2,1,0:T(8,128)(2,1)}), bf16[32,6,8,1024]{3,2,1,0:T(8,128)(2,1)S(1)}, u32[]{:S(2)}, u32[]{:S(2)}) async-start(bf16[32,6,8,1024]{3,2,1,0:T(8,128)(2,1)} %copy-done.1), calls=%async_computation.2 | async-start | bytes 6291456 | tf_op jit(solution)/shard_map/all_to_all | solution.py:307
  90.7 1.9 copy-start.2
  92.6 1.2 copy-start.5
  93.8 1.2 copy-start.7
  109.9 1.3 copy-start.3
  163.3 53.5 %all-to-all-start.1 = ((bf16[32,4,4,8,256]{4,3,2,1,0:T(8,128)(2,1)}), bf16[32,4,4,8,256]{4,3,2,1,0:T(8,128)(2,1)}, u32[]{:S(2)}, u32[]{:S(2)}) async-start(bf16[32,4,4,8,256]{4,3,2,1,0:T(8,128)(2,1)} %copy-done.3), calls=%async_computation.1 | async-start | bytes 4194304 | tf_op jit(solution)/shard_map/all_to_all | solution.py:317
  166.8 1.2 copy-start.6
  168.1 1.2 copy-start.8
  184.1 1.3 copy-start.4
where the time goes:
time: 333 us; the launch traced here: 332 us
  blocking collectives  133 us (40%)
  Pallas kernels  97.2 us (29%)
  waiting for transfers between devices  83.5 us (25%)
  local copies, waits for them, and re-layouts  11.6 us (3%)
  starting transfers between devices  6.26 us (2%)
    all_to_all x1, blocking collectives, local(): x = lax.all_to_all(x, AXES, split_axis=0, concat_axis=0, tiled=True)  79.7 us
    pallas_call x1, Pallas kernels, precondition(): pl.pallas_call(functools.partial(filter_kernel, chunks), grid=(dirs, mode...  61.6 us
    all_to_all x1, blocking collectives, local(): lax.all_to_all(y, AXES, split_axis=0, concat_axis=0, tiled=True)  53.5 us
    all_to_all x1, waiting for transfers between devices, local(): x = lax.all_to_all(x, AXES, split_axis=0, concat_axis=0, tiled=True)  52.1 us
    all_to_all x1, waiting for transfers between devices, local(): lax.all_to_all(y, AXES, split_axis=0, concat_axis=0, tiled=True)  31.4 us
    pallas_call x2, Pallas kernels, kerr(): pl.pallas_call(kerr_kernel, grid=(blocks,), in_specs=[pl.BlockSpec((2, po...  29.7 us
    unnamed x18, local copies, waits for them, and re-layouts  11.6 us
  transfers between devices with their start and end apart: 2, of which 2 were waited for; matrix products, arithmetic and copies ran while one was open for 0% of the time, Pallas kernels for 9%

commit v1 on v0

--- a/solution.py
+++ b/solution.py
@@ -96,7 +96,7 @@
     return jnp.dot(left, right, preferred_element_type=jnp.float32)
 
 
-def kerr_kernel(table_ref, back_ref, x_ref, out_ref):
+def kerr_kernel(table_ref, back_ref, x_ref, *out_refs):
     groups, sets, rows, cols = x_ref.shape
     modes = groups * rows
     points = table_ref.shape[1]
@@ -126,15 +126,17 @@
                     dot16(back_high, high) + dot16(back_low, high) + dot16(back_high, low)
                 )
     for e in range(dirs):
-        out_ref[:, 2 * e, 0] = (
+        at = 2 * (e % (dirs // len(out_refs)))
+        out_ref = out_refs[e * len(out_refs) // dirs]
+        out_ref[:, at, 0] = (
             (-KERR_GAIN * totals[2 * e + 1]).reshape(groups, rows, cols).astype(jnp.bfloat16)
         )
-        out_ref[:, 2 * e + 1, 0] = (
+        out_ref[:, at + 1, 0] = (
             (KERR_GAIN * totals[2 * e]).reshape(groups, rows, cols).astype(jnp.bfloat16)
         )
 
 
-def kerr(table, back, x):
+def kerr(table, back, x, pieces):
     groups, sets, rows, cols = x.shape
     _, points, modes = table.shape
     blocks = cols // LEN
@@ -147,8 +149,10 @@
             pl.BlockSpec((2, modes, points), lambda i: (0, 0, 0)),
             pl.BlockSpec((groups, sets, rows, LEN), lambda i: (0, 0, 0, i)),
         ],
-        out_specs=pl.BlockSpec((groups, outs, 1, rows, LEN), lambda i: (0, 0, i, 0, 0)),
-        out_shape=jax.ShapeDtypeStruct((groups, outs, blocks, rows, LEN), jnp.bfloat16),
+        out_specs=[pl.BlockSpec((groups, outs // pieces, 1, rows, LEN), lambda i: (0, 0, i, 0, 0))]
+        * pieces,
+        out_shape=[jax.ShapeDtypeStruct((groups, outs // pieces, blocks, rows, LEN), jnp.bfloat16)]
+        * pieces,
         compiler_params=pltpu.CompilerParams(vmem_limit_bytes=40 * MIB),
         cost_estimate=pl.CostEstimate(
             flops=2 * (2 * sets + 3 * outs) * points * modes * cols,
@@ -178,10 +182,10 @@
 def filter_kernel(chunks, degree_ref, left_ref, right_ref, left_inv_ref, right_inv_ref, twc_ref, tws_ref, disp_ref,
                   dir_ref, *rest):
     kerr_refs = rest[:chunks]
-    out_ref, wide, rows = rest[chunks:]
+    out_ref, wide, rows = rest[-3:]
     modes = dir_ref.shape[2]
     sources, _, blocks = kerr_refs[0].shape[:3]
-    mode = pl.program_id(1)
+    mode = pl.program_id(0)
 
     @pl.when(mode == 0)
     def _():
@@ -269,22 +273,31 @@
     return mats + [jnp.asarray(t, jnp.float32) for t in rest]
 
 
-def precondition(mode_degree, direction, kerr_parts):
+def precondition(mode_degree, direction, which, kerr_parts, result):
     dirs, _, modes, time_all = direction.shape
     chunks = len(kerr_parts)
     sources, _, blocks = kerr_parts[0].shape[:3]
-    big = pl.BlockSpec((2, 2 * LEN, 2 * LEN), lambda e, m: (0, 0, 0))
-    small = pl.BlockSpec((LEN, LEN), lambda e, m: (0, 0))
-    wave = pl.BlockSpec((1, 2, modes, time_all), lambda e, m: (e, 0, 0, 0))
-    part = pl.BlockSpec((sources, 2, blocks, modes, LEN), lambda e, m: (0, e, 0, 0, 0))
+    big = pl.BlockSpec((2, 2 * LEN, 2 * LEN), lambda m: (0, 0, 0))
+    small = pl.BlockSpec((LEN, LEN), lambda m: (0, 0))
+    wave = pl.BlockSpec((1, 2, modes, time_all), lambda m: (which, 0, 0, 0))
+    parts = [
+        pl.BlockSpec(
+            (sources, 2, blocks, modes, LEN),
+            lambda m, at=which if p.shape[1] == 2 * dirs else 0: (0, at, 0, 0, 0),
+        )
+        for p in kerr_parts
+    ]
+    extra = [] if result is None else [result]
+    operands = [mode_degree, *filter_tables(), direction, *kerr_parts, *extra]
     return pl.pallas_call(
         functools.partial(filter_kernel, chunks),
-        grid=(dirs, modes),
+        grid=(modes,),
         in_specs=[pl.BlockSpec(memory_space=pltpu.SMEM)]
         + [big] * 4
         + [small] * 3
         + [wave]
-        + [part] * chunks,
+        + parts
+        + [pl.BlockSpec(memory_space=pl.ANY)] * len(extra),
         out_specs=wave,
         out_shape=jax.ShapeDtypeStruct(direction.shape, jnp.float32),
         scratch_shapes=[
@@ -292,8 +305,14 @@
             pltpu.VMEM((2, modes, LEN, LEN), jnp.float32),
         ],
         compiler_params=pltpu.CompilerParams(vmem_limit_bytes=56 * MIB),
+        input_output_aliases={len(operands) - 1: 0} if extra else {},
+        cost_estimate=pl.CostEstimate(
+            flops=24 * modes * (2 * LEN) ** 2 * LEN,
+            bytes_accessed=20 * modes * time_all,
+            transcendentals=0,
+        ),
         name="precondition",
-    )(mode_degree, *filter_tables(), direction, *kerr_parts)
+    )(*operands)
 
 
 def local(devices, cavity_field, direction, mode_degree):
@@ -302,20 +321,28 @@
     forward = split_table(table)
     back = split_table(table.T)
     fold = max(1, 8 // modes)
+    dirs = direction.shape[0]
+    parts = prep(cavity_field, direction, devices, CHUNKS)
     kerr_parts = []
-    for x in prep(cavity_field, direction, devices, CHUNKS):
+    for j, x in enumerate(parts):
         x = lax.all_to_all(x, AXES, split_axis=0, concat_axis=0, tiled=True)
         if fold > 1:
             n, sets, r, cols = x.shape
             x = x.reshape(n // fold, fold, sets, r, cols).transpose(0, 2, 1, 3, 4)
             x = x.reshape(n // fold, sets, fold * r, cols)
-        y = kerr(forward, back, x)
-        if fold > 1:
-            n, outs, blocks, r, cols = y.shape
-            y = y.reshape(n, outs, blocks, fold, r // fold, cols).transpose(0, 3, 1, 2, 4, 5)
-            y = y.reshape(n * fold, outs, blocks, r // fold, cols)
-        kerr_parts.append(lax.all_to_all(y, AXES, split_axis=0, concat_axis=0, tiled=True))
-    return precondition(mode_degree, direction, kerr_parts)
+        sent = []
+        for y in kerr(forward, back, x, dirs if j == len(parts) - 1 else 1):
+            if fold > 1:
+                n, outs, blocks, r, cols = y.shape
+                y = y.reshape(n, outs, blocks, fold, r // fold, cols).transpose(0, 3, 1, 2, 4, 5)
+                y = y.reshape(n * fold, outs, blocks, r // fold, cols)
+            sent.append(lax.all_to_all(y, AXES, split_axis=0, concat_axis=0, tiled=True))
+        kerr_parts.append(sent)
+    result = None
+    for e in range(dirs):
+        arrived = [sent[e % len(sent)] for sent in kerr_parts]
+        result = precondition(mode_degree, direction, e, arrived, result)
+    return result
 
 
 def solution(mesh):

time: 333 us -> 320 us (0.961)
  waiting for transfers between devices: 83.5 us -> 60.8 us
  Pallas kernels: 97.2 us -> 103 us
    all_to_all x1 -> x2, waiting for transfers between devices: 31.4 us -> 8.92 us  [local(): lax.all_to_all(y, AXES, split_axis=0, concat_axis=0, tiled=True)]
    pallas_call x1 -> x2, Pallas kernels: 61.6 us -> 67.2 us  [precondition(): pl.pallas_call(functools.partial(filter_kernel, chunks), grid=(modes,), i...]
    unnamed x18 -> x20, local copies, waits for them, and re-layouts: 11.6 us -> 12.2 us
  transfers between devices with their start and end apart: 2 -> 3, of which waited for: 2 -> 2; matrix products, arithmetic and copies ran while one was open for 0% -> 0% of each run, Pallas kernels for 9% -> 20%
where the time goes in v1:
time: 320 us; the launch traced here: 319 us
  blocking collectives  133 us (42%)
  Pallas kernels  103 us (32%)
  waiting for transfers between devices  60.8 us (19%)
  local copies, waits for them, and re-layouts  12.2 us (4%)
  starting transfers between devices  8.99 us (3%)
    all_to_all x1, blocking collectives, local(): x = lax.all_to_all(x, AXES, split_axis=0, concat_axis=0, tiled=True)  79.7 us
    pallas_call x2, Pallas kernels, precondition(): pl.pallas_call(functools.partial(filter_kernel, chunks), grid=(modes,), i...  67.2 us
    all_to_all x1, blocking collectives, local(): lax.all_to_all(y, AXES, split_axis=0, concat_axis=0, tiled=True)  53.5 us
    all_to_all x1, waiting for transfers between devices, local(): x = lax.all_to_all(x, AXES, split_axis=0, concat_axis=0, tiled=True)  51.9 us
    pallas_call x2, Pallas kernels, kerr(): pl.pallas_call(kerr_kernel, grid=(blocks,), in_specs=[pl.BlockSpec((2, po...  30.3 us
    unnamed x20, local copies, waits for them, and re-layouts  12.2 us
    all_to_all x2, waiting for transfers between devices, local(): lax.all_to_all(y, AXES, split_axis=0, concat_axis=0, tiled=True)  8.92 us
  transfers between devices with their start and end apart: 3, of which 2 were waited for; matrix products, arithmetic and copies ran while one was open for 0% of the time, Pallas kernels for 20%

profile of v1, /device:TPU:0, one launch (start us, length us, event | category | flops | bytes accessed | tf_op | source)
XLA Modules:
  0.0 318.8 jit_solution(3131361420666432552)
XLA Ops:
  0.0 0.0 copy-start
  0.0 2.2 copy-done
  2.2 5.9 %prep.1 = (bf16[32,6,8,1024]{3,2,1,0:T(8,128)(2,1)S(1)}, bf16[32,6,8,1024]{3,2,1,0:T(8,128)(2,1)S(1)}) custom-call(f32[2,8,65536]{2,1,0:T(8,128)S(1)} %copy-done, f32[2,2,8,65536]{3,2,1,0:T(8,128)} %dir_ref.5), custom_call_target="tpu_custom_call" | custom-call | tf_op jit(solution)/shard_map/prep/pallas_call | solution.py:76
  8.1 0.0 copy-start.1
  8.1 79.7 %all_to_all.25.x_ref = bf16[32,6,8,1024]{3,2,1,0:T(8,128)(2,1)} all-to-all(bf16[32,6,8,1024]{3,2,1,0:T(8,128)(2,1)S(1)} %get-tuple-element.10), channel_id=1, replica_groups=mesh['grp'=4,'loc'=8] {'grp','loc'}, dimensions={0} | all-to-all | bytes 6291456 | tf_op jit(solution)/shard_map/all_to_all | solution.py:328
  87.9 0.0 copy-done.1
  87.9 2.8 all-to-all-start
  90.7 0.0 copy-start.2
  90.7 1.9 copy-done.2
  92.6 0.0 copy-start.5
  92.6 1.2 copy-done.5
  93.8 0.0 copy-start.7
  93.8 1.2 copy-done.7
  95.0 15.5 %kerr.3 = (bf16[32,2,4,8,256]{4,3,2,1,0:T(8,128)(2,1)S(1)}, bf16[32,2,4,8,256]{4,3,2,1,0:T(8,128)(2,1)}) custom-call(bf16[2,1024,256]{2,1,0:T(8,128)(2,1)S(1)} %copy-done.7, bf16[2,256,1024]{2,1,0:T(8,128)(2,1)S(1)} %copy-done.5, bf16[32,6,8,1024]{3,2,1,0:T(8,128)(2,1)S(1)} %copy-done.2), custom_call_target="tpu_custom_call" | custom-call | flops 12884901888 | bytes 5242880 | tf_op jit(solution)/shard_map/kerr/pallas_call | solution.py:144
  110.5 0.0 copy-start.4
  110.5 1.0 copy-done.4
  111.5 51.9 %all-to-all-done.x_ref = bf16[32,6,8,1024]{3,2,1,0:T(8,128)(2,1)S(1)} async-done(((bf16[32,6,8,1024]{3,2,1,0:T(8,128)(2,1)}), bf16[32,6,8,1024]{3,2,1,0:T(8,128)(2,1)S(1)}, u32[]{:S(2)}, u32[]{:S(2)}) %all-to-all-start) | async-done | bytes 3145760 | tf_op jit(solution)/shard_map/all_to_all | solution.py:328
  163.3 3.4 %all-to-all-start.4 = ((bf16[32,2,4,8,256]{4,3,2,1,0:T(8,128)(2,1)}), bf16[32,2,4,8,256]{4,3,2,1,0:T(8,128)(2,1)}, u32[]{:S(2)}, u32[]{:S(2)}) async-start(bf16[32,2,4,8,256]{4,3,2,1,0:T(8,128)(2,1)} %copy-done.4), calls=%async_computation.4 | async-start | bytes 2097152 | tf_op jit(solution)/shard_map/all_to_all | solution.py:339
  166.7 0.0 copy-start.6
  166.7 1.2 copy-done.6
  168.0 0.0 copy-start.8
  168.0 1.2 copy-done.8
  169.2 14.9 %kerr.2 = bf16[32,4,4,8,256]{4,3,2,1,0:T(8,128)(2,1)S(1)} custom-call(bf16[2,1024,256]{2,1,0:T(8,128)(2,1)S(1)} %copy-done.8, bf16[2,256,1024]{2,1,0:T(8,128)(2,1)S(1)} %copy-done.6, bf16[32,6,8,1024]{3,2,1,0:T(8,128)(2,1)S(1)} %all-to-all-done.x_ref), custom_call_target="tpu_custom_call" | custom-call | flops 12884901888 | bytes 5242880 | tf_op jit(solution)/shard_map/kerr/pallas_call | solution.py:144
  184.0 0.0 copy-start.3
  184.1 1.3 copy-done.3
  185.4 8.9 %all-to-all-done.4.rest_1_ = bf16[32,2,4,8,256]{4,3,2,1,0:T(8,128)(2,1)} async-done(((bf16[32,2,4,8,256]{4,3,2,1,0:T(8,128)(2,1)}), bf16[32,2,4,8,256]{4,3,2,1,0:T(8,128)(2,1)}, u32[]{:S(2)}, u32[]{:S(2)}) %all-to-all-start.4) | async-done | bytes 1048608 | tf_op jit(solution)/shard_map/all_to_all | solution.py:339
  194.3 53.5 %all_to_all.26.rest_0_ = bf16[32,4,4,8,256]{4,3,2,1,0:T(8,128)(2,1)} all-to-all(bf16[32,4,4,8,256]{4,3,2,1,0:T(8,128)(2,1)} %copy-done.3), channel_id=1, replica_groups=mesh['grp'=4,'loc'=8] {'grp','loc'}, dimensions={0} | all-to-all | bytes 4194304 | tf_op jit(solution)/shard_map/all_to_all | solution.py:339
  247.8 2.8 all-to-all-start.3
  250.6 33.6 %precondition.2.rest_2_ = f32[2,2,8,65536]{3,2,1,0:T(8,128)} custom-call(s32[8]{0:T(128)} %degree_ref.3, bf16[2,512,512]{2,1,0:T(8,128)(2,1)} %constant.16.clone.left_ref.right_inv_ref, bf16[2,512,512]{2,1,0:T(8,128)(2,1)} %constant.17.clone.right_ref.left_inv_ref, bf16[2,512,512]{2,1,0:T(8,128)(2,1)} %constant.17.clone.right_ref.left_inv_ref, ...), custom_call_target="tpu_custom_call" | custom-call | flops 12884901888 | bytes 10485760 | tf_op jit(solution)/shard_map/precondition/pallas_call | solution.py:292
  284.3 0.0 all-to-all-done.3.rest_1_
  284.3 1.0 copy-done.9
  285.2 33.5 %precondition.3 = f32[2,2,8,65536]{3,2,1,0:T(8,128)} custom-call(s32[8]{0:T(128)} %degree_ref.3, bf16[2,512,512]{2,1,0:T(8,128)(2,1)} %constant.16.clone.left_ref.right_inv_ref, bf16[2,512,512]{2,1,0:T(8,128)(2,1)} %constant.17.clone.right_ref.left_inv_ref, ...), custom_call_target="tpu_custom_call", output_to_operand_aliasing={{}: (11, {})} | custom-call | flops 12884901888 | bytes 10485760 | tf_op jit(solution)/shard_map/precondition/pallas_call | solution.py:292
  (1 shorter events, 0.0 us)
Async XLA Ops:
  0.0 2.2 copy-start
  8.1 79.8 %copy-start.1 = (bf16[32,6,8,1024]{3,2,1,0:T(8,128)(2,1)}, bf16[32,6,8,1024]{3,2,1,0:T(8,128)(2,1)S(1)}, u32[]{:S(2)}) copy-start(bf16[32,6,8,1024]{3,2,1,0:T(8,128)(2,1)S(1)} %get-tuple-element.9) | copy-start | bytes 9437188
  87.9 75.4 %all-to-all-start = ((bf16[32,6,8,1024]{3,2,1,0:T(8,128)(2,1)}), bf16[32,6,8,1024]{3,2,1,0:T(8,128)(2,1)S(1)}, u32[]{:S(2)}, u32[]{:S(2)}) async-start(bf16[32,6,8,1024]{3,2,1,0:T(8,128)(2,1)} %copy-done.1), calls=%async_computation | async-start | bytes 6291456 | tf_op jit(solution)/shard_map/all_to_all | solution.py:328
  90.7 1.9 copy-start.2
  92.6 1.2 copy-start.5
  93.8 1.2 copy-start.7
  110.5 1.0 copy-start.4
  163.3 31.0 %all-to-all-start.4 = ((bf16[32,2,4,8,256]{4,3,2,1,0:T(8,128)(2,1)}), bf16[32,2,4,8,256]{4,3,2,1,0:T(8,128)(2,1)}, u32[]{:S(2)}, u32[]{:S(2)}) async-start(bf16[32,2,4,8,256]{4,3,2,1,0:T(8,128)(2,1)} %copy-done.4), calls=%async_computation.4 | async-start | bytes 2097152 | tf_op jit(solution)/shard_map/all_to_all | solution.py:339
  166.7 1.2 copy-start.6
  168.0 1.2 copy-start.8
  184.0 1.3 copy-start.3
  247.8 36.5 %all-to-all-start.3 = ((bf16[32,2,4,8,256]{4,3,2,1,0:T(8,128)(2,1)}), bf16[32,2,4,8,256]{4,3,2,1,0:T(8,128)(2,1)S(1)}, u32[]{:S(2)}, u32[]{:S(2)}) async-start(bf16[32,2,4,8,256]{4,3,2,1,0:T(8,128)(2,1)} %get-tuple-element.11), calls=%async_computation.3 | async-start | bytes 2097152 | tf_op jit(solution)/shard_map/all_to_all | solution.py:339
  284.3 1.0 copy-start.9
